TPU v7x, 512 devices: a whole 4x8x8 slice. The times are simulated.
512 devices in a mesh: ctx: 64 (over x, z, core), tp: 8 (over y).
Axes of the slice: x: 4, y: 8, z: 8, core: 2. Of those that a mesh axis runs over, the one named last changes fastest.
Arguments:
- queries: bfloat16 [128, 8192], P('ctx', 'tp'), may hold values from -140 to 140
- cache_keys: bfloat16 [65536, 1024], P('ctx', 'tp'), may hold values from -6 to 6
- cache_values: bfloat16 [65536, 1024], P('ctx', 'tp'), may hold values from -6 to 6
- reply_keys: bfloat16 [128, 1024], P('ctx', 'tp'), may hold values from -6 to 6
- reply_values: bfloat16 [128, 1024], P('ctx', 'tp'), may hold values from -6 to 6
- block_prompt: int32 [64], P('ctx'), may hold values from 0 to 1, as said below
- lengths: int32 [4], replicated, may hold values from 1 to 64, 128 in all
- residual: bfloat16 [128, 8192], P(None, 'ctx'), may hold values from -6 to 6
- norm_gain: float32 [8192], P('ctx'), may hold values from 0.5 to 1.5
- out_weight: bfloat16 [8192, 8192], P('tp', 'ctx'), may hold values from -0.0625 to 0.0625
- vocab_weight: bfloat16 [8192, 16384], P('ctx', 'tp'), may hold values from -0.2 to 0.2
- targets: int32 [128], P('ctx'), may hold values from 0 to 16383
Outputs:
- slab_lse: float32 [128], P('ctx')
- target_logit: float32 [128], P('ctx')
Inputs may be any that keep to these rules, and one draw needn't show every extreme that they name: `block_prompt`: each prompt owns exactly 32 blocks.
All inputs are finite; a program needn't handle non-finite values.
Results may differ from a plain program's by a relative error of at most 0.0085.
Values may be sent and summed in bfloat16 or wider, within the bound.
A program may use at most 192 MiB of HBM per device.

v0:
```python
import jax
import jax.numpy as jnp
from jax import lax
from jax.sharding import PartitionSpec as P

D = 8192
HD = 128


NEG = -1e30
EPS = 1e-06


def combined_all(value, axis, join):
    pieces = jax.tree.map(lambda part: lax.all_gather(part, axis), value)
    head = jax.tree.map(lambda part: part[0], pieces)
    tail = jax.tree.map(lambda part: part[1:], pieces)
    so_far, _ = lax.scan(lambda so_far, slab: (join(so_far, slab), None), head, tail)
    return so_far


def contract(left, right):
    return lax.dot_general(
        left, right, (((1,), (1,)), ((), ())), preferred_element_type=jnp.float32
    )


def join_partials(first, second):
    top = jnp.maximum(first[0], second[0])
    left = jnp.exp(first[0] - top)
    right = jnp.exp(second[0] - top)
    total = first[1] * left + second[1] * right
    values = first[2] * left[..., None] + second[2] * right[..., None]
    return (top, total, values)


def body(
    queries,
    cache_keys,
    cache_values,
    reply_keys,
    reply_values,
    block_prompt,
    lengths,
    residual,
    norm_gain,
    out_weight,
    vocab_weight,
    targets,
):
    share = queries.shape[0]
    total_rows = share * lax.axis_size("ctx")
    position = lax.axis_index("ctx")
    gathered = lax.all_gather(queries, "ctx", axis=0, tiled=True)
    ends = jnp.cumsum(lengths)
    rows = jnp.arange(total_rows, dtype=jnp.int32)
    segment = jnp.sum((rows[:, None] >= ends[None, :]).astype(jnp.int32), axis=1)
    prompt = segment // 2
    own_rows = position * share + jnp.arange(share, dtype=jnp.int32)
    own_segment = lax.dynamic_slice_in_dim(segment, position * share, share)
    cache_mask = (prompt == block_prompt[0])[:, None]
    reply_mask = (segment[:, None] == own_segment[None, :]) & (own_rows[None, :] <= rows[:, None])
    local_heads = gathered.shape[1] // HD
    scale = HD ** (-0.5)

    def one_head(index):
        query = lax.dynamic_slice_in_dim(gathered, index * HD, HD, 1)
        first = jnp.where(cache_mask, contract(query, cache_keys) * scale, NEG)
        second = jnp.where(reply_mask, contract(query, reply_keys) * scale, NEG)
        top = jnp.maximum(jnp.max(first, axis=1), jnp.max(second, axis=1))
        pfirst = jnp.where(cache_mask, jnp.exp(first - top[:, None]), 0.0)
        psecond = jnp.where(reply_mask, jnp.exp(second - top[:, None]), 0.0)
        total = jnp.sum(pfirst, axis=1) + jnp.sum(psecond, axis=1)
        acc = jnp.dot(pfirst.astype(jnp.bfloat16), cache_values, preferred_element_type=jnp.float32)
        acc = acc + jnp.dot(
            psecond.astype(jnp.bfloat16), reply_values, preferred_element_type=jnp.float32
        )
        return (top, total, acc)

    top, total, acc = lax.map(one_head, jnp.arange(local_heads, dtype=jnp.int32))
    top, total, acc = combined_all((top, total, acc), "ctx", join_partials)
    attention = (acc / total[..., None]).astype(jnp.bfloat16)
    weight = out_weight.reshape(local_heads, HD, out_weight.shape[1])
    terms = jnp.einsum("hrd,hdc->rc", attention, weight, preferred_element_type=jnp.float32)
    mixed = lax.psum(terms.astype(jnp.bfloat16), "tp").astype(jnp.float32)
    hidden = residual.astype(jnp.float32) + mixed
    squares = lax.psum(jnp.sum(hidden * hidden, axis=1), "ctx")
    normed = (hidden * lax.rsqrt(squares / D + EPS)[:, None] * norm_gain[None, :]).astype(
        jnp.bfloat16
    )
    logits = lax.psum_scatter(
        jnp.dot(normed, vocab_weight, preferred_element_type=jnp.float32),
        "ctx",
        scatter_dimension=0,
        tiled=True,
    )
    width = logits.shape[1]
    columns = lax.axis_index("tp") * width + jnp.arange(width, dtype=jnp.int32)
    picked = jnp.sum(jnp.where(columns[None, :] == targets[:, None], logits, 0.0), axis=1)
    local_top = jnp.max(logits, axis=1)
    highest = lax.pmax(local_top, "tp")
    sums = jnp.sum(jnp.exp(logits - highest[:, None]), axis=1)
    sums, target_logit = lax.psum((sums, picked), "tp")
    slab_lse = highest + jnp.log(sums)
    return (slab_lse, target_logit)


def solution(mesh):
    return jax.shard_map(
        body,
        mesh=mesh,
        in_specs=(
            P("ctx", "tp"),
            P("ctx", "tp"),
            P("ctx", "tp"),
            P("ctx", "tp"),
            P("ctx", "tp"),
            P("ctx"),
            P(),
            P(None, "ctx"),
            P("ctx"),
            P("tp", "ctx"),
            P("ctx", "tp"),
            P("ctx"),
        ),
        out_specs=(P("ctx"), P("ctx")),
        check_vma=False,
    )
```

profile of v0, /device:TPU:4, one launch (start us, length us, event | category | flops | bytes accessed | tf_op | source)
XLA Modules:
  0.0 765.5 jit_solution(3072165265102817914)
XLA Ops:
  9.0 48.7 %all-gather.3 = bf16[64,2,1024]{2,1,0:T(2,128)(2,1)S(1)} all-gather(bf16[1,2,1024]{2,1,0:T(2,128)(2,1)} %bitcast.83), channel_id=1, replica_groups=mesh['ctx'=64,'tp'=8] {'ctx'}, dimensions={0}, use_global_device_ids=true | all-gather | bytes 266240 | tf_op jit(solution)/shard_map/all_gather | solution.py:54
  57.8 53.6 %while.30 = (s32[]{:T(128)}, f32[8,128]{1,0:T(8,128)S(1)}, f32[8,128]{1,0:T(8,128)S(1)}, f32[8,128,128]{2,1,0:T(8,128)}, pred[128,1]{0,1:T(4,128)(4,1)S(1)}, /*i...) while((s32[]{:T(128)}, f32[8,128]{1,0:T(8,128)S(1)}, ...), condition=%wide.region_7.8_spmd.clone, body=%wide.region_2.7_spmd.clone.sunk | while | flops 68440320 | bytes 2376719 | solution.py:80
  62.6 1.6 fusion.65
  69.3 1.6 fusion.65
  76.0 1.6 fusion.65
  82.7 1.6 fusion.65
  89.4 1.6 fusion.65
  96.1 1.6 fusion.65
  102.8 1.6 fusion.65
  109.5 1.6 fusion.65
  111.5 43.4 %all-gather = f32[512,128]{1,0:T(8,128)S(1)} all-gather(f32[8,128]{1,0:T(8,128)S(1)} %get-tuple-element.104), channel_id=2, replica_groups=mesh['ctx'=64,'tp'=8] {'ctx'}, dimensions={0}, use_global_device_ids=true | all-gather | bytes 266240 | tf_op jit(solution)/shard_map/all_gather | solution.py:15
  154.9 41.8 %all-gather.1 = f32[512,128]{1,0:T(8,128)S(1)} all-gather(f32[8,128]{1,0:T(8,128)S(1)} %get-tuple-element.105), channel_id=3, replica_groups=mesh['ctx'=64,'tp'=8] {'ctx'}, dimensions={0}, use_global_device_ids=true | all-gather | bytes 266240 | tf_op jit(solution)/shard_map/all_gather | solution.py:15
  196.8 59.7 %all-gather.6.cloned.1.call-done = f32[512,128,128]{2,1,0:T(8,128)} async-done(((f32[8,128,128]{2,1,0:T(8,128)}), f32[512,128,128]{2,1,0:T(8,128)}) %all-gather.6.cloned.1.call-update) | async-done | bytes 33554448 | tf_op jit(solution)/shard_map/all_gather | solution.py:15
  256.6 23.1 %slice.35 = f32[504,128,128]{2,1,0:T(8,128)} slice(f32[512,128,128]{2,1,0:T(8,128)} %all-gather.6.cloned.1.call-done), slice={[8:512], [0:128], [0:128]} | slice | bytes 66060288 | tf_op jit(solution)/shard_map/slice | solution.py:17
  279.7 98.2 %while.29 = (s32[]{:T(128)}, f32[8,128]{1,0:T(8,128)S(1)}, f32[8,128]{1,0:T(8,128)S(1)}, f32[8,128,128]{2,1,0:T(8,128)S(1)}, f32[63,8,128]{2,1,0:T(8,128)S(1)}, ...) while((s32[]{:T(128)}, f32[8,128]{1,0:T(8,128)S(1)}, f32[8,128]{1,0:T(8,128)S(1)}, ...), condition=%wide.region_9.10_spmd, body=%wide.region_8.9_spmd.sunk | while | flops 399362 | bytes 1613917 | solution.py:18
  279.7 1.5 fusion.53
  281.2 1.5 fusion.53
  282.8 1.5 fusion.53
  284.3 1.5 fusion.53
  285.9 1.5 fusion.53
  287.5 1.5 fusion.53
  289.0 1.5 fusion.53
  290.6 1.5 fusion.53
  292.1 1.5 fusion.53
  293.7 1.5 fusion.53
  295.3 1.5 fusion.53
  296.8 1.5 fusion.53
  298.4 1.5 fusion.53
  299.9 1.5 fusion.53
  301.5 1.5 fusion.53
  303.1 1.5 fusion.53
  304.6 1.5 fusion.53
  306.2 1.5 fusion.53
  307.7 1.5 fusion.53
  309.3 1.5 fusion.53
  310.8 1.5 fusion.53
  312.4 1.5 fusion.53
  314.0 1.5 fusion.53
  315.5 1.5 fusion.53
  317.1 1.5 fusion.53
  318.6 1.5 fusion.53
  340.5 1.5 fusion.53
  370.1 1.5 fusion.53
  378.2 29.8 %psum.28 = bf16[128,128]{1,0:T(8,128)(2,1)S(1)} all-reduce(bf16[128,128]{1,0:T(8,128)(2,1)S(1)} %fusion.23), channel_id=1, replica_groups=mesh['ctx'=64,'tp'=8] {'tp'}, use_global_device_ids=true, to_apply=%region_10.11 | all-reduce | flops 16384 | bytes 65536 | tf_op jit(solution)/shard_map/psum | solution.py:85
  408.1 104.7 %psum.29 = f32[128]{0:T(128)S(1)} all-reduce(f32[128]{0:T(128)S(1)} %multiply_reduce_fusion), channel_id=1, replica_groups=mesh['ctx'=64,'tp'=8] {'ctx'}, use_global_device_ids=true, to_apply=%region_12.13 | all-reduce | flops 128 | bytes 1024 | tf_op jit(solution)/shard_map/psum | solution.py:87
  516.1 207.3 %all-reduce.4.cloned.1.call-done = f32[128,2048]{1,0:T(8,128)} async-done(((f32[128,2048]{1,0:T(8,128)}), f32[128,2048]{1,0:T(8,128)}) %all-reduce.4.cloned.1.call-update) | async-done | bytes 1048592
  724.3 17.0 %pmax.7 = f32[2]{0:T(128)S(1)} all-reduce(f32[2]{0:T(128)S(1)} %dynamic-slice_reduce_fusion), channel_id=1, replica_groups=mesh['ctx'=64,'tp'=8] {'tp'}, use_global_device_ids=true, to_apply=%region_15.16 | all-reduce | flops 2 | bytes 16 | tf_op jit(solution)/shard_map/pmax | solution.py:101
  742.4 15.7 %all-reduce.1 = (f32[2]{0:T(128)S(1)}, f32[2]{0:T(128)}) all-reduce(f32[2]{0:T(128)S(1)} %get-tuple-element.143, f32[2]{0:T(128)S(1)} %get-tuple-element.142), channel_id=1, replica_groups=mesh['ctx'=64,'tp'=8] {'tp'}, use_global_device_ids=true, to_apply=%region_17.18 | all-reduce | flops 4 | bytes 32 | tf_op jit(solution)/shard_map/psum | solution.py:103
  (217 shorter events, 96.4 us)
Async XLA Ops:
  7.2 505.6 %copy-start = (bf16[128,2048]{1,0:T(8,128)(2,1)S(1)}, bf16[128,2048]{1,0:T(8,128)(2,1)}, u32[]{:S(2)}) copy-start(bf16[128,2048]{1,0:T(8,128)(2,1)} %param.26) | copy-start | bytes 1572868
  7.2 249.4 %all-gather.6.cloned.1.call-start = ((), (), s32[]{:S(2)}) async-start(), calls=%async_computation | async-start | bytes 34078720 | tf_op jit(solution)/shard_map/all_gather | solution.py:15
  111.5 611.9 %all-reduce.4.cloned.1.call-start = ((), (), s32[]{:S(2)}) async-start(), calls=%async_computation.1 | async-start | bytes 2097152
  196.8 181.1 %copy-start.4 = (bf16[1024,128]{1,0:T(8,128)(2,1)S(1)}, bf16[1024,128]{1,0:T(8,128)(2,1)}, u32[]{:S(2)}) copy-start(bf16[1024,128]{1,0:T(8,128)(2,1)} %param.25) | copy-start | bytes 786436
  196.8 211.2 %copy-start.1 = (bf16[128,128]{1,0:T(8,128)(2,1)S(1)}, bf16[128,128]{1,0:T(8,128)(2,1)}, u32[]{:S(2)}) copy-start(bf16[128,128]{1,0:T(8,128)(2,1)} %param.23) | copy-start | bytes 98308
  196.8 316.0 %copy-start.2 = (f32[128]{0:T(128)S(1)}, f32[128]{0:T(128)}, u32[]{:S(2)}) copy-start(f32[128]{0:T(128)} %param.24) | copy-start | bytes 1540
  196.8 544.5 %copy-start.3 = (s32[2]{0:T(128)S(1)}, s32[2]{0:T(128)}, u32[]{:S(2)}) copy-start(s32[2]{0:T(128)} %param.27) | copy-start | bytes 28
  256.6 23.1 %slice-start = ((f32[512,128,128]{2,1,0:T(8,128)}), f32[8,128,128]{2,1,0:T(8,128)S(1)}, s32[]{:S(2)}) async-start(f32[512,128,128]{2,1,0:T(8,128)} %all-gather.6.cloned.1.call-done), calls=%async_computation.2 | async-start | bytes 1048576 | tf_op jit(solution)/shard_map/slice | solution.py:16
Sparse Core Ops, SparseCore 0:
  111.6 144.9 all-gather.5
  514.3 209.0 all-reduce.3
where the time goes:
time: 770 us; the launch traced here: 765 us
  blocking collectives  301 us (39%)
  waiting for transfers between devices  267 us (35%)
  other arithmetic  103 us (13%)
  matrix products  40.9 us (5%)
  local copies, waits for them, and re-layouts  30.5 us (4%)
  between operations  15.5 us (2%)
    unnamed x3, waiting for transfers between devices  207 us
    psum x1, blocking collectives, body(): squares = lax.psum(jnp.sum(hidden * hidden, axis=1), 'ctx')  105 us
    add x63, other arithmetic, join_partials(): values = first[2] * left[..., None] + second[2] * right[..., None]  95.7 us
    all_gather x2, blocking collectives, combined_all(): pieces = jax.tree.map(lambda part: lax.all_gather(part, axis), value)  85.2 us
    all_gather x1, waiting for transfers between devices, combined_all(): pieces = jax.tree.map(lambda part: lax.all_gather(part, axis), value)  59.7 us
    all_gather x1, blocking collectives, body(): gathered = lax.all_gather(queries, 'ctx', axis=0, tiled=True)  48.7 us
    psum x1, blocking collectives, body(): mixed = lax.psum(terms.astype(jnp.bfloat16), 'tp').astype(jnp.float32)  29.8 us
    slice x3, local copies, waits for them, and re-layouts, combined_all(): tail = jax.tree.map(lambda part: part[1:], pieces)  23.1 us
  transfers between devices with their start and end apart: 2, of which 2 were waited for; matrix products, arithmetic and copies ran while one was open for 0% of the time, Pallas kernels for 0%

commit v1 on v0

v1 whole, which is shorter than its diff:
```python
import functools

import jax
import jax.numpy as jnp
from jax import lax
from jax.experimental import pallas as pl
from jax.experimental.pallas import tpu as pltpu
from jax.sharding import PartitionSpec as P

MESH = pl.DeviceIdType.MESH
F32 = jnp.float32
BF16 = jnp.bfloat16

HD = 128
HEADS = 8
NEG = -1e30
EPS = 1e-06
LOG2E = 1.4426950408889634
LANES = 128
CHUNK = 128


def iota(shape, dim):
    return lax.broadcasted_iota(jnp.int32, shape, dim)


def dot(a, b):
    return jnp.dot(a, b, preferred_element_type=F32)


def dot_t(a, b):
    return lax.dot_general(a, b, (((1,), (1,)), ((), ())), preferred_element_type=F32)


def roll_rows(x, shift, period):
    if shift % period == 0:
        return x
    shift = shift % period
    return jnp.concatenate([x[:, shift:], x[:, :shift]], axis=1)


def kernel(
    plane,
    ny,
    width,
    q_hbm,
    k_hbm,
    v_hbm,
    rk_hbm,
    rv_hbm,
    bp_smem,
    len_smem,
    res_hbm,
    gain_hbm,
    w_hbm,
    vw_hbm,
    tgt_smem,
    out_ref,
    q_in,
    rk_in,
    rv_in,
    gain_in,
    kbuf,
    vbuf,
    resbuf,
    wbuf,
    vwbuf,
    misc,
    qbuf,
    tsrc,
    tbuf,
    perm,
    acc_s,
    acc_r,
    st_s,
    st_r,
    abuf,
    t_s,
    t_r,
    hbuf,
    l_s,
    l_r,
    s2_s,
    s2_r,
    f_r,
    local_sem,
    send_sem,
    recv_sem,
):
    ctx = lax.axis_index("ctx")
    y = lax.axis_index("tp")
    core = ctx % 2
    me = ctx // 2
    partner = (ctx + 1 - 2 * core, y)
    nctx = 2 * plane
    rows = 2 * plane
    qrows = 16 * plane
    groups = plane // 4
    features = nctx * LANES
    keys = kbuf.shape[1]
    c1 = (HD ** (-0.5)) * LOG2E

    def plane_peers():
        return [((ctx + 2 * k) % nctx, y) for k in range(1, plane)]

    def y_peers():
        return [(ctx, (y + k) % ny) for k in range(1, ny)]

    barrier = pltpu.get_barrier_semaphore()
    greeted = [partner] + plane_peers() + y_peers()
    for peer in greeted:
        pl.semaphore_signal(barrier, inc=1, device_id=peer, device_id_type=MESH)

    def local(index, src, dst):
        copy = pltpu.make_async_copy(src, dst, local_sem.at[index])
        copy.start()
        return copy

    copies = [
        local(0, q_hbm, q_in),
        local(1, rk_hbm, rk_in),
        local(2, rv_hbm, rv_in),
        local(3, gain_hbm, gain_in),
    ]
    big = [
        local(4, k_hbm, kbuf.at[0]),
        local(5, v_hbm, vbuf.at[0]),
        local(6, res_hbm, resbuf.at[0]),
        local(7, w_hbm, wbuf.at[0]),
        local(8, vw_hbm, vwbuf.at[0:LANES]),
    ]
    for copy in copies:
        copy.wait()

    def send(index, src, dst, peer):
        pltpu.make_async_remote_copy(
            src_ref=src,
            dst_ref=dst,
            send_sem=send_sem.at[index],
            recv_sem=recv_sem.at[index],
            device_id=peer,
            device_id_type=MESH,
        ).start()

    def bytes_of(index, ref):
        return pltpu.make_async_remote_copy(
            src_ref=ref,
            dst_ref=ref,
            send_sem=send_sem.at[index],
            recv_sem=recv_sem.at[index],
            device_id=partner,
            device_id_type=MESH,
        )

    qf = q_in[...].astype(F32)
    tile = jnp.concatenate([qf[:, h * HD : (h + 1) * HD] for h in range(HEADS)], axis=0)
    qbuf[me] = tile.astype(BF16)
    misc[0, 0:1, :] = gain_in[...]
    misc[0, 1:2, :] = jnp.full((1, LANES), bp_smem[0], jnp.int32).astype(F32)
    misc[0, 2:4, :] = rk_in[...].astype(F32)
    misc[0, 4:6, :] = rv_in[...].astype(F32)
    misc[0, 6:8, :] = jnp.zeros((2, LANES), F32)
    two = iota((2, LANES), 0)
    tsrc[...] = jnp.where(two == 0, tgt_smem[0], tgt_smem[1])
    tbuf[me] = tsrc[...]

    pl.semaphore_wait(barrier, len(greeted))

    for peer in plane_peers():
        send(0, qbuf.at[me], qbuf.at[me], peer)
    send(1, misc.at[0], misc.at[1], partner)
    send(2, k_hbm, kbuf.at[1], partner)
    send(3, v_hbm, vbuf.at[1], partner)
    for peer in plane_peers():
        send(4, tsrc, tbuf.at[me], peer)
    send(5, res_hbm, resbuf.at[1], partner)
    send(6, w_hbm, wbuf.at[1], partner)
    send(7, vw_hbm, vwbuf.at[LANES : 2 * LANES], partner)

    for head in range(HEADS):
        into = iota((rows, qrows), 0)
        source = (into // 2) * 16 + head * 2 + into % 2
        perm[head * rows : (head + 1) * rows, :] = jnp.where(
            iota((rows, qrows), 1) == source, 1.0, 0.0
        ).astype(BF16)

    end0 = len_smem[0]
    end1 = end0 + len_smem[1]
    end2 = end1 + len_smem[2]

    def segment(index):
        one = lambda end: jnp.where(index >= end, 1, 0)
        return one(end0) + one(end1) + one(end2) + one(end2 + len_smem[3])

    for copy in big:
        copy.wait()
    bytes_of(1, misc.at[1]).wait_recv()
    bytes_of(2, kbuf.at[1]).wait_recv()
    bytes_of(3, vbuf.at[1]).wait_recv()

    own, other = misc[0], misc[1]
    fill = jnp.zeros((LANES - 4, HD), F32)
    rk = jnp.concatenate([own[2:4], other[2:4], fill], axis=0).astype(BF16)
    rv = jnp.concatenate([own[4:6], other[4:6], fill], axis=0).astype(BF16)
    prompts = (own[1:2, 0:1], other[1:2, 0:1])
    lane = iota((CHUNK, LANES), 1)
    key_row = jnp.where(lane < 2, 2 * ctx + lane, 2 * (ctx + 1 - 2 * core) + lane - 2)
    key_segment = segment(key_row)

    bytes_of(0, qbuf.at[0 : plane - 1]).wait_recv()

    def attend(chunk):
        first = chunk * CHUNK
        tiles = CHUNK // 16
        q = qbuf[chunk * tiles : (chunk + 1) * tiles].reshape(CHUNK, HD)
        n = first + iota((CHUNK, LANES), 0)
        row = 4 * (n // 16) + 2 * core + n % 2
        row_segment = segment(row)
        row_prompt = (row_segment // 2).astype(F32)
        parts = []
        for block in range(2):
            s = dot_t(q, kbuf[block])
            m = jnp.max(s, axis=1, keepdims=True)
            p = jnp.exp2((s - m) * c1)
            total = jnp.sum(p, axis=1, keepdims=True)
            acc = dot(p.astype(BF16), vbuf[block])
            m = jnp.where(row_prompt == prompts[block], m, NEG)
            parts.append((m, total, acc))
        allowed = (lane < 4) & (key_segment == row_segment) & (key_row <= row)
        s = jnp.where(allowed, dot_t(q, rk), NEG)
        m = jnp.max(s, axis=1, keepdims=True)
        p = jnp.where(allowed, jnp.exp2((s - m) * c1), 0.0)
        parts.append((m, jnp.sum(p, axis=1, keepdims=True), dot(p.astype(BF16), rv)))
        top = jnp.maximum(jnp.maximum(parts[0][0], parts[1][0]), parts[2][0])
        total = jnp.zeros((CHUNK, LANES), F32)
        acc = jnp.zeros((CHUNK, HD), F32)
        for m, t, a in parts:
            w = jnp.exp2((m - top) * c1)
            total = total + w * t
            acc = acc + w * a
        acc_s[chunk * tiles : (chunk + 1) * tiles] = acc.astype(BF16).reshape(tiles, 16, HD)
        here = lane == (me % 8) * 16 + n % 16
        for which, stat in ((0, top), (1, total)):
            packed = jnp.where(here, stat, 0.0).reshape(tiles, 16, LANES)
            st_s[chunk * tiles : (chunk + 1) * tiles, which : which + 1, :] = jnp.sum(
                packed, axis=1, keepdims=True
            )

    for chunk in range(qrows // CHUNK):
        attend(chunk)

    for k in range(1, plane):
        peer = ((ctx + 2 * k) % nctx, y)
        to = (me + k) % plane
        send(8, st_s.at[to], st_r.at[me], peer)
        send(9, acc_s.at[to], acc_r.at[me], peer)
    acc_r[me] = acc_s[me]
    st_r[me] = st_s[me]

    bytes_of(5, resbuf.at[1]).wait_recv()
    at = pl.multiple_of(y * 16, 16)
    around = jnp.concatenate(
        [resbuf[0, pl.ds(at, 16), :], resbuf[1, pl.ds(at, 16), :]], axis=0
    ).astype(F32)
    into = iota((16, 32), 0)
    inner = into % 8
    source = (into // 8) * 16 + 4 * (inner // 2) + 2 * core + inner % 2
    pick = jnp.where(iota((16, 32), 1) == source, 1.0, 0.0)
    residual = dot(pick.astype(BF16), around.astype(BF16))
    upper = iota((16, LANES), 0) < 8
    gain = jnp.where(upper, own[0:1], other[0:1])

    bytes_of(8, st_r.at[0 : plane - 1]).wait_recv()
    bytes_of(9, acc_r.at[0 : plane - 1]).wait_recv()

    stats = [jnp.sum(st_r[x * 8 : (x + 1) * 8], axis=0) for x in range(plane // 8)]
    m = jnp.concatenate([s[0:1] for s in stats], axis=0)
    total = jnp.concatenate([s[1:2] for s in stats], axis=0)

    def around_lanes(x, join):
        for shift in (16, 32, 64):
            x = join(x, pltpu.roll(x, shift, 1))
        return x

    top = around_lanes(jnp.max(m, axis=0, keepdims=True), jnp.maximum)
    w = jnp.exp2((m - top) * c1)
    total = around_lanes(jnp.sum(w * total, axis=0, keepdims=True), jnp.add)
    w = w / total
    diagonal = iota((16, LANES), 1) % 16 == iota((16, LANES), 0)
    w = jnp.concatenate(
        [jnp.where(diagonal, w[x : x + 1], 0.0) for x in range(plane // 8)], axis=1
    )
    high = w.astype(BF16)
    low = (w - high.astype(F32)).astype(BF16)
    partials = acc_r[...].reshape(qrows, HD)
    attention = dot(high, partials) + dot(low, partials)
    abuf[me] = attention.astype(BF16)
    for peer in plane_peers():
        send(10, abuf.at[me], abuf.at[me], peer)
    bytes_of(6, wbuf.at[1]).wait_recv()
    bytes_of(7, vwbuf.at[0:LANES]).wait_recv()
    bytes_of(4, tbuf.at[0 : plane - 1]).wait_recv()
    target = jnp.concatenate([tbuf[j] for j in range(plane)], axis=0).reshape(groups, 8, LANES)
    bytes_of(10, abuf.at[0 : plane - 1]).wait_recv()

    heads = dot(perm[...], abuf[...].reshape(qrows, HD)).astype(BF16)
    heads = jnp.concatenate([heads[h * rows : (h + 1) * rows] for h in range(HEADS)], axis=1)
    terms = [dot(heads, wbuf[half]).reshape(ny, 8, LANES) for half in range(2)]
    t_s[...] = jnp.concatenate(terms, axis=1).astype(BF16)
    for k in range(1, ny):
        to = (y + k) % ny
        send(11, t_s.at[to], t_r.at[y], (ctx, to))
    t_r[y] = t_s[y]
    bytes_of(11, t_r.at[0 : ny - 1]).wait_recv()
    mixed = jnp.sum(t_r[...].astype(F32), axis=0)
    hidden = residual + mixed
    hbuf[y] = (hidden * gain).astype(BF16)
    for peer in y_peers():
        send(12, hbuf.at[y], hbuf.at[y], peer)
    bytes_of(12, hbuf.at[0 : ny - 1]).wait_recv()

    gathered = hbuf[...].astype(F32)
    halves = [gathered[:, :8], gathered[:, 8:]]
    plain = [halves[0] / own[0:1], halves[1] / other[0:1]]
    squares = jnp.sum(plain[0] * plain[0] + plain[1] * plain[1], axis=2, keepdims=True)
    x = jnp.concatenate(halves, axis=2)

    span = width // 4
    blocks = span // LANES
    logits = []
    picked = jnp.zeros((groups, 8, 1), F32)
    for q in range(4):
        turned = roll_rows(x, 2 * q, 8).reshape(rows, 2 * LANES).astype(BF16)
        part = dot(turned, vwbuf[:, q * span : (q + 1) * span]).reshape(groups, 8, span)
        column = y * width + q * span + iota((groups, 8, span), 2)
        wanted = roll_rows(target, 2 * q, 8)[:, :, 0:1]
        found = jnp.sum(jnp.where(column == wanted, part, 0.0), axis=2, keepdims=True)
        picked = picked + roll_rows(found, -2 * q, 8)
        logits.append(part)
    pair = iota((groups, 8, LANES), 1) // 2
    for u in range(4):
        pieces = []
        for b in range(blocks):
            cut = [part[:, :, b * LANES : (b + 1) * LANES] for part in logits]
            piece = cut[(u - 3) % 4]
            for p in range(3):
                piece = jnp.where(pair == p, cut[(u - p) % 4], piece)
            pieces.append(piece)
        l_s[:, u] = jnp.concatenate(pieces, axis=1).astype(BF16)
    own_group, own_place = me // 4, me % 4
    for k in range(1, plane):
        peer = ((ctx + 2 * k) % nctx, y)
        to = (me + k) % plane
        send(13, l_s.at[to // 4, to % 4], l_r.at[me], peer)
    l_r[me] = l_s[own_group, own_place]
    both = jnp.where(iota((groups, 8, LANES), 2) < 64, squares, picked)
    for j in range(plane):
        s2_s[j] = both[j // 4, 2 * (j % 4) : 2 * (j % 4) + 2]
    for k in range(1, plane):
        peer = ((ctx + 2 * k) % nctx, y)
        send(14, s2_s.at[(me + k) % plane], s2_r.at[me], peer)
    s2_r[me] = s2_s[me]
    bytes_of(13, l_r.at[0 : plane - 1]).wait_recv()
    bytes_of(14, s2_r.at[0 : plane - 1]).wait_recv()

    total = jnp.sum(l_r[...].astype(F32), axis=0)
    both = jnp.sum(s2_r[...], axis=0)
    both = jnp.concatenate([both] * 4, axis=0)
    inverse = lax.rsqrt(both[:, 0:1] / features + EPS)
    picked = both[:, 64:65] * inverse
    logit = total.reshape(-1, 8, LANES) * inverse

    def around_pairs(x, join):
        x = jnp.broadcast_to(x, (8, LANES))
        for shift in (2, 4):
            x = join(x, pltpu.roll(x, shift, 0))
        return x

    top = around_pairs(jnp.max(jnp.max(logit, axis=0), axis=1, keepdims=True), jnp.maximum)
    sums = jnp.sum(jnp.sum(jnp.exp(logit - top), axis=0), axis=1, keepdims=True)
    sums = around_pairs(sums, jnp.add)
    lane8 = iota((8, LANES), 1)
    f_r[y] = jnp.where(lane8 < 32, top, jnp.where(lane8 < 64, sums, picked))
    for peer in y_peers():
        send(15, f_r.at[y], f_r.at[y], peer)
    bytes_of(15, f_r.at[0 : ny - 1]).wait_recv()
    final = f_r[...]
    tops = final[:, :, 0:1]
    top = jnp.max(tops, axis=0)
    sums = jnp.sum(final[:, :, 32:33] * jnp.exp(tops - top), axis=0)
    lse = top + jnp.log(sums)
    picked = jnp.sum(final[:, :, 64:65], axis=0)
    out_ref[...] = jnp.where(lane8 < 64, lse, picked)

    bytes_of(0, qbuf.at[0 : plane - 1]).wait_send()
    bytes_of(1, misc.at[1]).wait_send()
    bytes_of(2, kbuf.at[1]).wait_send()
    bytes_of(3, vbuf.at[1]).wait_send()
    bytes_of(4, tbuf.at[0 : plane - 1]).wait_send()
    bytes_of(5, resbuf.at[1]).wait_send()
    bytes_of(6, wbuf.at[1]).wait_send()
    bytes_of(7, vwbuf.at[0:LANES]).wait_send()
    bytes_of(8, st_r.at[0 : plane - 1]).wait_send()
    bytes_of(9, acc_r.at[0 : plane - 1]).wait_send()
    bytes_of(10, abuf.at[0 : plane - 1]).wait_send()
    bytes_of(11, t_r.at[0 : ny - 1]).wait_send()
    bytes_of(12, hbuf.at[0 : ny - 1]).wait_send()
    bytes_of(13, l_r.at[0 : plane - 1]).wait_send()
    bytes_of(14, s2_r.at[0 : plane - 1]).wait_send()
    bytes_of(15, f_r.at[0 : ny - 1]).wait_send()


def body(plane, ny, *args):
    (
        queries,
        cache_keys,
        cache_values,
        reply_keys,
        reply_values,
        block_prompt,
        lengths,
        residual,
        norm_gain,
        out_weight,
        vocab_weight,
        targets,
    ) = args
    width = vocab_weight.shape[1]
    keys = cache_keys.shape[0]
    rows = 2 * plane
    qrows = 16 * plane
    anywhere = pl.BlockSpec(memory_space=pl.ANY)
    smem = pl.BlockSpec(memory_space=pltpu.SMEM)
    vmem = pltpu.VMEM
    out = pl.pallas_call(
        functools.partial(kernel, plane, ny, width),
        out_shape=jax.ShapeDtypeStruct((8, LANES), F32),
        in_specs=[
            anywhere,
            anywhere,
            anywhere,
            anywhere,
            anywhere,
            smem,
            smem,
            anywhere,
            anywhere,
            anywhere,
            anywhere,
            smem,
        ],
        out_specs=pl.BlockSpec(memory_space=pltpu.VMEM),
        scratch_shapes=[
            vmem(queries.shape, BF16),
            vmem(reply_keys.shape, BF16),
            vmem(reply_values.shape, BF16),
            vmem((1, LANES), F32),
            vmem((2, keys, HD), BF16),
            vmem((2, keys, HD), BF16),
            vmem((2,) + residual.shape, BF16),
            vmem((2,) + out_weight.shape, BF16),
            vmem((2 * LANES, width), BF16),
            vmem((2, 8, LANES), F32),
            vmem((plane, 16, HD), BF16),
            vmem((2, LANES), jnp.int32),
            vmem((plane, 2, LANES), jnp.int32),
            vmem((qrows, qrows), BF16),
            vmem((plane, 16, HD), BF16),
            vmem((plane, 16, HD), BF16),
            vmem((plane, 2, LANES), F32),
            vmem((plane, 2, LANES), F32),
            vmem((plane, 16, HD), BF16),
            vmem((ny, 16, LANES), BF16),
            vmem((ny, 16, LANES), BF16),
            vmem((ny, 16, LANES), BF16),
            vmem((plane // 4, 4, 2 * width // LANES, LANES), BF16),
            vmem((plane, 2 * width // LANES, LANES), BF16),
            vmem((plane, 2, LANES), F32),
            vmem((plane, 2, LANES), F32),
            vmem((ny, 8, LANES), F32),
            pltpu.SemaphoreType.DMA((9,)),
            pltpu.SemaphoreType.DMA((16,)),
            pltpu.SemaphoreType.DMA((16,)),
        ],
        compiler_params=pltpu.CompilerParams(
            collective_id=0, has_side_effects=True, vmem_limit_bytes=40 * 2**20
        ),
    )(
        queries,
        cache_keys,
        cache_values,
        reply_keys,
        reply_values,
        block_prompt,
        lengths,
        residual,
        norm_gain.reshape(1, LANES),
        out_weight,
        vocab_weight,
        targets,
    )
    return out[0:2, 0], out[0:2, 64]


def solution(mesh):
    plane, ny = mesh.shape["ctx"] // 2, mesh.shape["tp"]
    return jax.shard_map(
        functools.partial(body, plane, ny),
        mesh=mesh,
        in_specs=(
            P("ctx", "tp"),
            P("ctx", "tp"),
            P("ctx", "tp"),
            P("ctx", "tp"),
            P("ctx", "tp"),
            P("ctx"),
            P(),
            P(None, "ctx"),
            P("ctx"),
            P("tp", "ctx"),
            P("ctx", "tp"),
            P("ctx"),
        ),
        out_specs=(P("ctx"), P("ctx")),
        check_vma=False,
    )
```

time: 770 us -> 73.9 us (0.10)
  the two profiles are of different devices: /device:TPU:4 before, /device:TPU:2 now
where the time goes in v1:
time: 73.9 us; the launch traced here: 73.6 us
  Pallas kernels  65.5 us (89%)
  local copies, waits for them, and re-layouts  6.68 us (9%)
  between operations  1.37 us (2%)
    pallas_call x1, Pallas kernels, body(): pl.pallas_call(functools.partial(kernel, plane, ny, width), out_shape=jax...  65.5 us
    unnamed x22, local copies, waits for them, and re-layouts  5.98 us

profile of v1, /device:TPU:2, one launch (start us, length us, event | category | flops | bytes accessed | tf_op | source)
XLA Modules:
  0.0 73.6 jit_solution(4621802784604780474)
XLA Ops:
  0.6 0.0 copy-start.9
  0.6 0.0 copy-start.10
  1.3 0.0 copy-start.6
  1.3 0.0 copy-start.7
  1.3 0.0 copy-start.8
  1.3 0.0 copy-done.9
  1.4 0.0 copy-done.10
  1.4 0.6 copy-done.6
  2.0 0.0 copy-done.7
  2.0 0.0 copy-done.8
  2.0 0.0 copy-start
  2.0 1.0 %copy-done = bf16[128,2048]{1,0:T(8,128)(2,1)S(1)} copy-done((bf16[128,2048]{1,0:T(8,128)(2,1)S(1)}, bf16[128,2048]{1,0:T(8,128)(2,1)}, u32[]{:S(2)}) %copy-start) | copy-done | bytes 524312
  3.0 0.0 copy-start.1
  3.1 0.9 %copy-done.1 = bf16[1024,128]{1,0:T(8,128)(2,1)S(1)} copy-done((bf16[1024,128]{1,0:T(8,128)(2,1)S(1)}, bf16[1024,128]{1,0:T(8,128)(2,1)}, u32[]{:S(2)}) %copy-start.1) | copy-done | bytes 262168
  4.0 0.0 copy-start.2
  4.0 0.9 %copy-done.2 = bf16[1024,128]{1,0:T(8,128)(2,1)S(1)} copy-done((bf16[1024,128]{1,0:T(8,128)(2,1)S(1)}, bf16[1024,128]{1,0:T(8,128)(2,1)}, u32[]{:S(2)}) %copy-start.2) | copy-done | bytes 262168
  5.0 0.0 copy-start.3
  5.0 0.9 %copy-done.3 = bf16[1024,128]{1,0:T(8,128)(2,1)S(1)} copy-done((bf16[1024,128]{1,0:T(8,128)(2,1)S(1)}, bf16[1024,128]{1,0:T(8,128)(2,1)}, u32[]{:S(2)}) %copy-start.3) | copy-done | bytes 262168
  5.9 0.0 copy-start.4
  5.9 0.8 %copy-done.4 = bf16[128,128]{1,0:T(8,128)(2,1)S(1)} copy-done((bf16[128,128]{1,0:T(8,128)(2,1)S(1)}, bf16[128,128]{1,0:T(8,128)(2,1)}, u32[]{:S(2)}) %copy-start.4) | copy-done | bytes 32792
  6.7 0.0 copy-start.5
  6.7 0.7 copy-done.5
  7.3 65.5 %shard_map.131 = f32[8,128]{1,0:T(8,128)S(1)} custom-call(bf16[2,1024]{1,0:T(2,128)(2,1)S(1)} %copy-done.5, bf16[1024,128]{1,0:T(8,128)(2,1)S(1)} %copy-done.1, bf16[1024,128]{1,0:T(8,128)(2,1)S(1)} %copy-done.2, bf16[2,128]{1,0:T(2,128)(2,1)S(1)} %copy-done.6, bf16[2,128]{1,0:T(2,128)(2,1)S(1)} %copy-done.7, s32[1]{0:T(128)S(6)} %copy.14.bp_smem, ...), custom_call_target="tpu_custom_call" | custom-call | tf_op jit(solution)/shard_map/pallas_call | solution.py:435
  72.9 0.7 slice_reduce_fusion
Async XLA Ops:
  0.6 0.7 copy-start.9
  0.6 0.7 copy-start.10
  1.3 0.7 copy-start.6
  1.3 0.7 copy-start.7
  1.3 0.7 copy-start.8
  2.0 1.0 %copy-start = (bf16[128,2048]{1,0:T(8,128)(2,1)S(1)}, bf16[128,2048]{1,0:T(8,128)(2,1)}, u32[]{:S(2)}) copy-start(bf16[128,2048]{1,0:T(8,128)(2,1)} %vw_hbm.1) | copy-start | bytes 1572868
  3.0 0.9 %copy-start.1 = (bf16[1024,128]{1,0:T(8,128)(2,1)S(1)}, bf16[1024,128]{1,0:T(8,128)(2,1)}, u32[]{:S(2)}) copy-start(bf16[1024,128]{1,0:T(8,128)(2,1)} %k_hbm.1) | copy-start | bytes 786436
  4.0 0.9 %copy-start.2 = (bf16[1024,128]{1,0:T(8,128)(2,1)S(1)}, bf16[1024,128]{1,0:T(8,128)(2,1)}, u32[]{:S(2)}) copy-start(bf16[1024,128]{1,0:T(8,128)(2,1)} %v_hbm.1) | copy-start | bytes 786436
  5.0 0.9 %copy-start.3 = (bf16[1024,128]{1,0:T(8,128)(2,1)S(1)}, bf16[1024,128]{1,0:T(8,128)(2,1)}, u32[]{:S(2)}) copy-start(bf16[1024,128]{1,0:T(8,128)(2,1)} %w_hbm.1) | copy-start | bytes 786436
  5.9 0.8 %copy-start.4 = (bf16[128,128]{1,0:T(8,128)(2,1)S(1)}, bf16[128,128]{1,0:T(8,128)(2,1)}, u32[]{:S(2)}) copy-start(bf16[128,128]{1,0:T(8,128)(2,1)} %res_hbm.1) | copy-start | bytes 98308
  6.7 0.7 copy-start.5

commit v2 on v1

--- a/solution.py
+++ b/solution.py
@@ -32,11 +32,9 @@
     return lax.dot_general(a, b, (((1,), (1,)), ((), ())), preferred_element_type=F32)
 
 
-def roll_rows(x, shift, period):
-    if shift % period == 0:
-        return x
-    shift = shift % period
-    return jnp.concatenate([x[:, shift:], x[:, :shift]], axis=1)
+def roll_rows(x, shift):
+    shift = shift % 8
+    return jnp.concatenate([x[shift:], x[:shift]], axis=0) if shift else x
 
 
 def kernel(
@@ -48,18 +46,21 @@
     v_hbm,
     rk_hbm,
     rv_hbm,
-    bp_smem,
-    len_smem,
+    bp_hbm,
+    len_hbm,
     res_hbm,
     gain_hbm,
     w_hbm,
     vw_hbm,
-    tgt_smem,
+    tgt_hbm,
     out_ref,
     q_in,
     rk_in,
     rv_in,
     gain_in,
+    bp_smem,
+    len_smem,
+    tgt_smem,
     kbuf,
     vbuf,
     resbuf,
@@ -69,7 +70,6 @@
     qbuf,
     tsrc,
     tbuf,
-    perm,
     acc_s,
     acc_r,
     st_s,
@@ -93,21 +93,23 @@
     me = ctx // 2
     partner = (ctx + 1 - 2 * core, y)
     nctx = 2 * plane
-    rows = 2 * plane
     qrows = 16 * plane
-    groups = plane // 4
     features = nctx * LANES
-    keys = kbuf.shape[1]
     c1 = (HD ** (-0.5)) * LOG2E
 
-    def plane_peers():
-        return [((ctx + 2 * k) % nctx, y) for k in range(1, plane)]
-
-    def y_peers():
-        return [(ctx, (y + k) % ny) for k in range(1, ny)]
+    nz = 8
+    nx = plane // nz
+    along_x = [((me // nz + dx) % nx) * nz for dx in range(nx)]
+    along_z = [(me % nz + dz) % nz for dz in range(nz)]
+    steps = [(dx, dz) for dx in range(nx) for dz in range(nz) if dx or dz]
+    steps.sort(key=lambda s: -min(s[0], nx - s[0]) - min(s[1], nz - s[1]))
+    plane_to = [along_x[dx] + along_z[dz] for dx, dz in steps]
+    plane_peers = [(to, (2 * to + core, y)) for to in plane_to]
+    y_steps = sorted(range(1, ny), key=lambda s: -min(s, ny - s))
+    y_peers = [((y + k) % ny, (ctx, (y + k) % ny)) for k in y_steps]
 
     barrier = pltpu.get_barrier_semaphore()
-    greeted = [partner] + plane_peers() + y_peers()
+    greeted = [device for _, device in plane_peers + y_peers] + [partner]
     for peer in greeted:
         pl.semaphore_signal(barrier, inc=1, device_id=peer, device_id_type=MESH)
 
@@ -121,6 +123,9 @@
         local(1, rk_hbm, rk_in),
         local(2, rv_hbm, rv_in),
         local(3, gain_hbm, gain_in),
+        local(9, bp_hbm, bp_smem),
+        local(10, len_hbm, len_smem),
+        local(11, tgt_hbm, tgt_smem),
     ]
     big = [
         local(4, k_hbm, kbuf.at[0]),
@@ -166,23 +171,18 @@
 
     pl.semaphore_wait(barrier, len(greeted))
 
-    for peer in plane_peers():
-        send(0, qbuf.at[me], qbuf.at[me], peer)
+    for (dx, _), (_, peer) in zip(steps, plane_peers):
+        send(16 + dx, qbuf.at[me], qbuf.at[me], peer)
     send(1, misc.at[0], misc.at[1], partner)
     send(2, k_hbm, kbuf.at[1], partner)
     send(3, v_hbm, vbuf.at[1], partner)
-    for peer in plane_peers():
-        send(4, tsrc, tbuf.at[me], peer)
     send(5, res_hbm, resbuf.at[1], partner)
     send(6, w_hbm, wbuf.at[1], partner)
     send(7, vw_hbm, vwbuf.at[LANES : 2 * LANES], partner)
 
-    for head in range(HEADS):
-        into = iota((rows, qrows), 0)
-        source = (into // 2) * 16 + head * 2 + into % 2
-        perm[head * rows : (head + 1) * rows, :] = jnp.where(
-            iota((rows, qrows), 1) == source, 1.0, 0.0
-        ).astype(BF16)
+    into = iota((nz * 16, nz * 16), 0)
+    source = (into // 2 % nz) * 16 + (into // (2 * nz)) * 2 + into % 2
+    perm = jnp.where(iota((nz * 16, nz * 16), 1) == source, 1.0, 0.0).astype(BF16)
 
     end0 = len_smem[0]
     end1 = end0 + len_smem[1]
@@ -207,12 +207,11 @@
     key_row = jnp.where(lane < 2, 2 * ctx + lane, 2 * (ctx + 1 - 2 * core) + lane - 2)
     key_segment = segment(key_row)
 
-    bytes_of(0, qbuf.at[0 : plane - 1]).wait_recv()
-
-    def attend(chunk):
-        first = chunk * CHUNK
-        tiles = CHUNK // 16
-        q = qbuf[chunk * tiles : (chunk + 1) * tiles].reshape(CHUNK, HD)
+    tiles = CHUNK // 16
+
+    def attend(at):
+        first = at * 16
+        q = qbuf[pl.ds(at, tiles)].reshape(CHUNK, HD)
         n = first + iota((CHUNK, LANES), 0)
         row = 4 * (n // 16) + 2 * core + n % 2
         row_segment = segment(row)
@@ -238,22 +237,21 @@
             w = jnp.exp2((m - top) * c1)
             total = total + w * t
             acc = acc + w * a
-        acc_s[chunk * tiles : (chunk + 1) * tiles] = acc.astype(BF16).reshape(tiles, 16, HD)
+        acc_s[pl.ds(at, tiles)] = acc.astype(BF16).reshape(tiles, 16, HD)
         here = lane == (me % 8) * 16 + n % 16
         for which, stat in ((0, top), (1, total)):
             packed = jnp.where(here, stat, 0.0).reshape(tiles, 16, LANES)
-            st_s[chunk * tiles : (chunk + 1) * tiles, which : which + 1, :] = jnp.sum(
+            st_s[pl.ds(at, tiles), which : which + 1, :] = jnp.sum(
                 packed, axis=1, keepdims=True
             )
 
-    for chunk in range(qrows // CHUNK):
-        attend(chunk)
-
-    for k in range(1, plane):
-        peer = ((ctx + 2 * k) % nctx, y)
-        to = (me + k) % plane
-        send(8, st_s.at[to], st_r.at[me], peer)
-        send(9, acc_s.at[to], acc_r.at[me], peer)
+    for dx in sorted(range(nx), key=lambda d: min(d, nx - d) if d != nx - 1 else nx):
+        bytes_of(16 + dx, qbuf.at[0 : nz - (dx == 0)]).wait_recv()
+        attend(along_x[(nx - dx) % nx])
+        for (back, _), (to, peer) in zip(steps, plane_peers):
+            if back == (nx - dx) % nx:
+                send(8, st_s.at[to], st_r.at[me], peer)
+                send(9, acc_s.at[to], acc_r.at[me], peer)
     acc_r[me] = acc_s[me]
     st_r[me] = st_s[me]
 
@@ -295,70 +293,81 @@
     partials = acc_r[...].reshape(qrows, HD)
     attention = dot(high, partials) + dot(low, partials)
     abuf[me] = attention.astype(BF16)
-    for peer in plane_peers():
-        send(10, abuf.at[me], abuf.at[me], peer)
+    for (dx, _), (_, peer) in zip(steps, plane_peers):
+        send(4 if dx == 0 else 27 + dx, abuf.at[me], abuf.at[me], peer)
+    for _, peer in plane_peers:
+        send(0, tsrc, tbuf.at[me], peer)
     bytes_of(6, wbuf.at[1]).wait_recv()
     bytes_of(7, vwbuf.at[0:LANES]).wait_recv()
-    bytes_of(4, tbuf.at[0 : plane - 1]).wait_recv()
-    target = jnp.concatenate([tbuf[j] for j in range(plane)], axis=0).reshape(groups, 8, LANES)
-    bytes_of(10, abuf.at[0 : plane - 1]).wait_recv()
-
-    heads = dot(perm[...], abuf[...].reshape(qrows, HD)).astype(BF16)
-    heads = jnp.concatenate([heads[h * rows : (h + 1) * rows] for h in range(HEADS)], axis=1)
-    terms = [dot(heads, wbuf[half]).reshape(ny, 8, LANES) for half in range(2)]
-    t_s[...] = jnp.concatenate(terms, axis=1).astype(BF16)
-    for k in range(1, ny):
-        to = (y + k) % ny
-        send(11, t_s.at[to], t_r.at[y], (ctx, to))
+
+    share = ny // nx
+    for dx in sorted(range(nx), key=lambda d: min(d, nx - d)):
+        bytes_of(4 if dx == 0 else 27 + dx, abuf.at[0 : nz - (dx == 0)]).wait_recv()
+        at = along_x[(nx - dx) % nx]
+        heads = dot(perm, abuf[pl.ds(at, nz)].reshape(nz * 16, HD)).astype(BF16)
+        span = 2 * nz
+        heads = jnp.concatenate([heads[h * span : (h + 1) * span] for h in range(HEADS)], axis=1)
+        terms = [dot(heads, wbuf[half]).reshape(share, 8, LANES) for half in range(2)]
+        to = at // nz * share
+        t_s[pl.ds(to, share)] = jnp.concatenate(terms, axis=1).astype(BF16)
+        for k in range(share):
+            pl.when(to + k != y)(
+                lambda to=to + k: send(11, t_s.at[to], t_r.at[y], (ctx, to))
+            )
     t_r[y] = t_s[y]
     bytes_of(11, t_r.at[0 : ny - 1]).wait_recv()
     mixed = jnp.sum(t_r[...].astype(F32), axis=0)
     hidden = residual + mixed
     hbuf[y] = (hidden * gain).astype(BF16)
-    for peer in y_peers():
-        send(12, hbuf.at[y], hbuf.at[y], peer)
-    bytes_of(12, hbuf.at[0 : ny - 1]).wait_recv()
-
-    gathered = hbuf[...].astype(F32)
-    halves = [gathered[:, :8], gathered[:, 8:]]
-    plain = [halves[0] / own[0:1], halves[1] / other[0:1]]
-    squares = jnp.sum(plain[0] * plain[0] + plain[1] * plain[1], axis=2, keepdims=True)
-    x = jnp.concatenate(halves, axis=2)
+    for k, (_, peer) in zip(y_steps, y_peers):
+        send(19 + k, hbuf.at[y], hbuf.at[y], peer)
+    bytes_of(0, tbuf.at[0 : plane - 1]).wait_recv()
 
     span = width // 4
     blocks = span // LANES
-    logits = []
-    picked = jnp.zeros((groups, 8, 1), F32)
-    for q in range(4):
-        turned = roll_rows(x, 2 * q, 8).reshape(rows, 2 * LANES).astype(BF16)
-        part = dot(turned, vwbuf[:, q * span : (q + 1) * span]).reshape(groups, 8, span)
-        column = y * width + q * span + iota((groups, 8, span), 2)
-        wanted = roll_rows(target, 2 * q, 8)[:, :, 0:1]
-        found = jnp.sum(jnp.where(column == wanted, part, 0.0), axis=2, keepdims=True)
-        picked = picked + roll_rows(found, -2 * q, 8)
-        logits.append(part)
-    pair = iota((groups, 8, LANES), 1) // 2
-    for u in range(4):
-        pieces = []
-        for b in range(blocks):
-            cut = [part[:, :, b * LANES : (b + 1) * LANES] for part in logits]
-            piece = cut[(u - 3) % 4]
-            for p in range(3):
-                piece = jnp.where(pair == p, cut[(u - p) % 4], piece)
-            pieces.append(piece)
-        l_s[:, u] = jnp.concatenate(pieces, axis=1).astype(BF16)
-    own_group, own_place = me // 4, me % 4
-    for k in range(1, plane):
-        peer = ((ctx + 2 * k) % nctx, y)
-        to = (me + k) % plane
-        send(13, l_s.at[to // 4, to % 4], l_r.at[me], peer)
-    l_r[me] = l_s[own_group, own_place]
-    both = jnp.where(iota((groups, 8, LANES), 2) < 64, squares, picked)
-    for j in range(plane):
-        s2_s[j] = both[j // 4, 2 * (j % 4) : 2 * (j % 4) + 2]
-    for k in range(1, plane):
-        peer = ((ctx + 2 * k) % nctx, y)
-        send(14, s2_s.at[(me + k) % plane], s2_r.at[me], peer)
+    pair = iota((8, LANES), 0) // 2
+    for dy in sorted(range(ny), key=lambda d: min(d, ny - d)):
+        if dy:
+            bytes_of(19 + dy, hbuf.at[0]).wait_recv()
+        group = (y + ny - dy) % ny
+        gathered = hbuf[group].astype(F32)
+        halves = [gathered[:8], gathered[8:]]
+        plain = [halves[0] / own[0:1], halves[1] / other[0:1]]
+        squares = jnp.sum(plain[0] * plain[0] + plain[1] * plain[1], axis=1, keepdims=True)
+        x = jnp.concatenate(halves, axis=1)
+        turned = jnp.concatenate([roll_rows(x, 2 * q) for q in range(4)], axis=0).astype(BF16)
+        product = dot(turned, vwbuf[...])
+        marks = tbuf[pl.ds(group * 4, 4)]
+        target = jnp.concatenate([marks[u] for u in range(4)], axis=0)
+        logits = []
+        picked = jnp.zeros((8, 1), F32)
+        for q in range(4):
+            part = product[8 * q : 8 * q + 8, q * span : (q + 1) * span]
+            column = y * width + q * span + iota((8, span), 1)
+            wanted = roll_rows(target, 2 * q)[:, 0:1]
+            found = jnp.sum(jnp.where(column == wanted, part, 0.0), axis=1, keepdims=True)
+            picked = picked + roll_rows(found, -2 * q)
+            logits.append(part)
+        both = jnp.where(iota((8, LANES), 1) < 64, squares, picked)
+        for u in range(4):
+            pieces = []
+            for b in range(blocks):
+                cut = [part[:, b * LANES : (b + 1) * LANES] for part in logits]
+                piece = cut[(u - 3) % 4]
+                for p in range(3):
+                    piece = jnp.where(pair == p, cut[(u - p) % 4], piece)
+                pieces.append(piece)
+            l_s[group, u] = jnp.concatenate(pieces, axis=0).astype(BF16)
+            to = group * 4 + u
+            s2_s[to] = both[2 * u : 2 * u + 2]
+
+            @pl.when(to != me)
+            def _(u=u, to=to, group=group):
+                peer = (2 * to + core, y)
+                send(13, l_s.at[group, u], l_r.at[me], peer)
+                send(14, s2_s.at[to], s2_r.at[me], peer)
+
+    l_r[me] = l_s[me // 4, me % 4]
     s2_r[me] = s2_s[me]
     bytes_of(13, l_r.at[0 : plane - 1]).wait_recv()
     bytes_of(14, s2_r.at[0 : plane - 1]).wait_recv()
@@ -381,7 +390,7 @@
     sums = around_pairs(sums, jnp.add)
     lane8 = iota((8, LANES), 1)
     f_r[y] = jnp.where(lane8 < 32, top, jnp.where(lane8 < 64, sums, picked))
-    for peer in y_peers():
+    for _, peer in y_peers:
         send(15, f_r.at[y], f_r.at[y], peer)
     bytes_of(15, f_r.at[0 : ny - 1]).wait_recv()
     final = f_r[...]
@@ -392,19 +401,21 @@
     picked = jnp.sum(final[:, :, 64:65], axis=0)
     out_ref[...] = jnp.where(lane8 < 64, lse, picked)
 
-    bytes_of(0, qbuf.at[0 : plane - 1]).wait_send()
+    for dx in range(nx):
+        bytes_of(16 + dx, qbuf.at[0 : nz - (dx == 0)]).wait_send()
+        bytes_of(4 if dx == 0 else 27 + dx, abuf.at[0 : nz - (dx == 0)]).wait_send()
+    for k in range(1, ny):
+        bytes_of(19 + k, hbuf.at[0]).wait_send()
     bytes_of(1, misc.at[1]).wait_send()
     bytes_of(2, kbuf.at[1]).wait_send()
     bytes_of(3, vbuf.at[1]).wait_send()
-    bytes_of(4, tbuf.at[0 : plane - 1]).wait_send()
+    bytes_of(0, tbuf.at[0 : plane - 1]).wait_send()
     bytes_of(5, resbuf.at[1]).wait_send()
     bytes_of(6, wbuf.at[1]).wait_send()
     bytes_of(7, vwbuf.at[0:LANES]).wait_send()
     bytes_of(8, st_r.at[0 : plane - 1]).wait_send()
     bytes_of(9, acc_r.at[0 : plane - 1]).wait_send()
-    bytes_of(10, abuf.at[0 : plane - 1]).wait_send()
     bytes_of(11, t_r.at[0 : ny - 1]).wait_send()
-    bytes_of(12, hbuf.at[0 : ny - 1]).wait_send()
     bytes_of(13, l_r.at[0 : plane - 1]).wait_send()
     bytes_of(14, s2_r.at[0 : plane - 1]).wait_send()
     bytes_of(15, f_r.at[0 : ny - 1]).wait_send()
@@ -427,34 +438,21 @@
     ) = args
     width = vocab_weight.shape[1]
     keys = cache_keys.shape[0]
-    rows = 2 * plane
-    qrows = 16 * plane
-    anywhere = pl.BlockSpec(memory_space=pl.ANY)
-    smem = pl.BlockSpec(memory_space=pltpu.SMEM)
+    hbm = pl.BlockSpec(memory_space=pltpu.HBM)
     vmem = pltpu.VMEM
     out = pl.pallas_call(
         functools.partial(kernel, plane, ny, width),
         out_shape=jax.ShapeDtypeStruct((8, LANES), F32),
-        in_specs=[
-            anywhere,
-            anywhere,
-            anywhere,
-            anywhere,
-            anywhere,
-            smem,
-            smem,
-            anywhere,
-            anywhere,
-            anywhere,
-            anywhere,
-            smem,
-        ],
+        in_specs=[hbm] * len(args),
         out_specs=pl.BlockSpec(memory_space=pltpu.VMEM),
         scratch_shapes=[
             vmem(queries.shape, BF16),
             vmem(reply_keys.shape, BF16),
             vmem(reply_values.shape, BF16),
             vmem((1, LANES), F32),
+            pltpu.SMEM(block_prompt.shape, jnp.int32),
+            pltpu.SMEM(lengths.shape, jnp.int32),
+            pltpu.SMEM(targets.shape, jnp.int32),
             vmem((2, keys, HD), BF16),
             vmem((2, keys, HD), BF16),
             vmem((2,) + residual.shape, BF16),
@@ -464,7 +462,6 @@
             vmem((plane, 16, HD), BF16),
             vmem((2, LANES), jnp.int32),
             vmem((plane, 2, LANES), jnp.int32),
-            vmem((qrows, qrows), BF16),
             vmem((plane, 16, HD), BF16),
             vmem((plane, 16, HD), BF16),
             vmem((plane, 2, LANES), F32),
@@ -478,12 +475,12 @@
             vmem((plane, 2, LANES), F32),
             vmem((plane, 2, LANES), F32),
             vmem((ny, 8, LANES), F32),
-            pltpu.SemaphoreType.DMA((9,)),
-            pltpu.SemaphoreType.DMA((16,)),
-            pltpu.SemaphoreType.DMA((16,)),
+            pltpu.SemaphoreType.DMA((12,)),
+            pltpu.SemaphoreType.DMA((32,)),
+            pltpu.SemaphoreType.DMA((32,)),
         ],
         compiler_params=pltpu.CompilerParams(
-            collective_id=0, has_side_effects=True, vmem_limit_bytes=40 * 2**20
+            collective_id=0, has_side_effects=True, vmem_limit_bytes=60 * 2**20
         ),
     )(
         queries,

time: 73.9 us -> 62.8 us (0.85)
  the two profiles are of different devices: /device:TPU:2 before, /device:TPU:8 now
where the time goes in v2:
time: 62.8 us; the launch traced here: 62.6 us
  Pallas kernels  59.8 us (95%)
  local copies, waits for them, and re-layouts  1.49 us (2%)
  between operations  1.29 us (2%)
    pallas_call x1, Pallas kernels, body(): pl.pallas_call(functools.partial(kernel, plane, ny, width), out_shape=jax...  59.8 us
    slice x1, local copies, waits for them, and re-layouts, body(): return (out[0:2, 0], out[0:2, 64])  1.49 us

profile of v2, /device:TPU:8, one launch (start us, length us, event | category | flops | bytes accessed | tf_op | source)
XLA Modules:
  0.0 62.6 jit_solution(4317534246861085399)
XLA Ops:
  1.3 59.8 %shard_map.131 = f32[8,128]{1,0:T(8,128)} custom-call(bf16[2,1024]{1,0:T(2,128)(2,1)} %q_hbm.1, bf16[1024,128]{1,0:T(8,128)(2,1)} %k_hbm.1, bf16[1024,128]{1,0:T(8,128)(2,1)} %v_hbm.1, bf16[2,128]{1,0:T(2,128)(2,1)} %rk_hbm.1, bf16[2,128]{1,0:T(2,128)(2,1)} %rv_hbm.1, s32[1]{0:T(128)S(6)} %copy.14.bp_hbm, s32[4]{0:T(128)} %len_hbm.1, ...), custom_call_target="tpu_custom_call" | custom-call | tf_op jit(solution)/shard_map/pallas_call | solution.py:443
  61.1 1.5 %slice_reduce_fusion = (f32[2]{0:T(128)}, f32[2]{0:T(128)}) fusion(f32[8,128]{1,0:T(8,128)} %shard_map.131), kind=kLoop, calls=%fused_computation | loop fusion | bytes 32 | tf_op jit(solution)/shard_map/slice | solution.py:499

commit v3 on v2

--- a/solution.py
+++ b/solution.py
@@ -255,16 +255,17 @@
     acc_r[me] = acc_s[me]
     st_r[me] = st_s[me]
 
+    half = ny // 2
     bytes_of(5, resbuf.at[1]).wait_recv()
-    at = pl.multiple_of(y * 16, 16)
-    around = jnp.concatenate(
-        [resbuf[0, pl.ds(at, 16), :], resbuf[1, pl.ds(at, 16), :]], axis=0
-    ).astype(F32)
     into = iota((16, 32), 0)
     inner = into % 8
     source = (into // 8) * 16 + 4 * (inner // 2) + 2 * core + inner % 2
-    pick = jnp.where(iota((16, 32), 1) == source, 1.0, 0.0)
-    residual = dot(pick.astype(BF16), around.astype(BF16))
+    pick = jnp.where(iota((16, 32), 1) == source, 1.0, 0.0).astype(BF16)
+    residual = []
+    for group in (y, (y + half) % ny):
+        at = pl.multiple_of(group * 16, 16)
+        around = [resbuf[side, pl.ds(at, 16), :] for side in range(2)]
+        residual.append(dot(pick, jnp.concatenate(around, axis=0)))
     upper = iota((16, LANES), 0) < 8
     gain = jnp.where(upper, own[0:1], other[0:1])
 
@@ -311,26 +312,33 @@
         to = at // nz * share
         t_s[pl.ds(to, share)] = jnp.concatenate(terms, axis=1).astype(BF16)
         for k in range(share):
-            pl.when(to + k != y)(
-                lambda to=to + k: send(11, t_s.at[to], t_r.at[y], (ctx, to))
-            )
-    t_r[y] = t_s[y]
-    bytes_of(11, t_r.at[0 : ny - 1]).wait_recv()
-    mixed = jnp.sum(t_r[...].astype(F32), axis=0)
-    hidden = residual + mixed
-    hbuf[y] = (hidden * gain).astype(BF16)
-    for k, (_, peer) in zip(y_steps, y_peers):
-        send(19 + k, hbuf.at[y], hbuf.at[y], peer)
+            for slot in range(2):
+                owner = (to + k + slot * half) % ny
+
+                @pl.when(owner != y)
+                def _(group=to + k, slot=slot, owner=owner):
+                    send(11, t_s.at[group], t_r.at[slot * ny + y], (ctx, owner))
+
+    for slot in range(2):
+        t_r[slot * ny + y] = t_s[(y + slot * half) % ny]
+    bytes_of(11, t_r.at[0 : 2 * (ny - 1)]).wait_recv()
+    for slot in range(2):
+        mixed = jnp.sum(t_r[slot * ny : (slot + 1) * ny].astype(F32), axis=0)
+        hbuf[y, slot] = ((residual[slot] + mixed) * gain).astype(BF16)
+    offsets = sorted(range(1 - half // 2, half // 2 + 1), key=abs)
+    for k in range(half - 1, 0, -1):
+        send(19 + k, hbuf.at[y], hbuf.at[y], (ctx, (y + ny + offsets[k]) % ny))
     bytes_of(0, tbuf.at[0 : plane - 1]).wait_recv()
 
     span = width // 4
     blocks = span // LANES
     pair = iota((8, LANES), 0) // 2
-    for dy in sorted(range(ny), key=lambda d: min(d, ny - d)):
-        if dy:
-            bytes_of(19 + dy, hbuf.at[0]).wait_recv()
-        group = (y + ny - dy) % ny
-        gathered = hbuf[group].astype(F32)
+    for k, slot in [(k, slot) for k in range(half) for slot in range(2)]:
+        if k and slot == 0:
+            bytes_of(19 + k, hbuf.at[0]).wait_recv()
+        owner = (y + ny - offsets[k]) % ny
+        group = (owner + slot * half) % ny
+        gathered = hbuf[owner, slot].astype(F32)
         halves = [gathered[:8], gathered[8:]]
         plain = [halves[0] / own[0:1], halves[1] / other[0:1]]
         squares = jnp.sum(plain[0] * plain[0] + plain[1] * plain[1], axis=1, keepdims=True)
@@ -392,19 +400,10 @@
     f_r[y] = jnp.where(lane8 < 32, top, jnp.where(lane8 < 64, sums, picked))
     for _, peer in y_peers:
         send(15, f_r.at[y], f_r.at[y], peer)
-    bytes_of(15, f_r.at[0 : ny - 1]).wait_recv()
-    final = f_r[...]
-    tops = final[:, :, 0:1]
-    top = jnp.max(tops, axis=0)
-    sums = jnp.sum(final[:, :, 32:33] * jnp.exp(tops - top), axis=0)
-    lse = top + jnp.log(sums)
-    picked = jnp.sum(final[:, :, 64:65], axis=0)
-    out_ref[...] = jnp.where(lane8 < 64, lse, picked)
-
     for dx in range(nx):
         bytes_of(16 + dx, qbuf.at[0 : nz - (dx == 0)]).wait_send()
         bytes_of(4 if dx == 0 else 27 + dx, abuf.at[0 : nz - (dx == 0)]).wait_send()
-    for k in range(1, ny):
+    for k in range(1, half):
         bytes_of(19 + k, hbuf.at[0]).wait_send()
     bytes_of(1, misc.at[1]).wait_send()
     bytes_of(2, kbuf.at[1]).wait_send()
@@ -415,9 +414,18 @@
     bytes_of(7, vwbuf.at[0:LANES]).wait_send()
     bytes_of(8, st_r.at[0 : plane - 1]).wait_send()
     bytes_of(9, acc_r.at[0 : plane - 1]).wait_send()
-    bytes_of(11, t_r.at[0 : ny - 1]).wait_send()
+    bytes_of(11, t_r.at[0 : 2 * (ny - 1)]).wait_send()
     bytes_of(13, l_r.at[0 : plane - 1]).wait_send()
     bytes_of(14, s2_r.at[0 : plane - 1]).wait_send()
+    bytes_of(15, f_r.at[0 : ny - 1]).wait_recv()
+    final = f_r[...]
+    tops = final[:, :, 0:1]
+    top = jnp.max(tops, axis=0)
+    sums = jnp.sum(final[:, :, 32:33] * jnp.exp(tops - top), axis=0)
+    lse = top + jnp.log(sums)
+    picked = jnp.sum(final[:, :, 64:65], axis=0)
+    out_ref[...] = jnp.where(lane8 < 64, lse, picked)
+
     bytes_of(15, f_r.at[0 : ny - 1]).wait_send()
 
 
@@ -468,8 +476,8 @@
             vmem((plane, 2, LANES), F32),
             vmem((plane, 16, HD), BF16),
             vmem((ny, 16, LANES), BF16),
-            vmem((ny, 16, LANES), BF16),
-            vmem((ny, 16, LANES), BF16),
+            vmem((2 * ny, 16, LANES), BF16),
+            vmem((ny, 2, 16, LANES), BF16),
             vmem((plane // 4, 4, 2 * width // LANES, LANES), BF16),
             vmem((plane, 2 * width // LANES, LANES), BF16),
             vmem((plane, 2, LANES), F32),

time: 62.8 us -> 61.8 us (0.984)
  Pallas kernels: 59.8 us -> 58.8 us
    pallas_call x1, Pallas kernels: 59.8 us -> 58.8 us  [body(): pl.pallas_call(functools.partial(kernel, plane, ny, width), out_shape=jax...]
where the time goes in v3:
time: 61.8 us; the launch traced here: 61.6 us
  Pallas kernels  58.8 us (95%)
  local copies, waits for them, and re-layouts  1.49 us (2%)
  between operations  1.29 us (2%)
    pallas_call x1, Pallas kernels, body(): pl.pallas_call(functools.partial(kernel, plane, ny, width), out_shape=jax...  58.8 us
    slice x1, local copies, waits for them, and re-layouts, body(): return (out[0:2, 0], out[0:2, 64])  1.49 us

profile of v3, /device:TPU:8, one launch (start us, length us, event | category | flops | bytes accessed | tf_op | source)
XLA Modules:
  0.0 61.6 jit_solution(15789752386280861170)
XLA Ops:
  1.3 58.8 %shard_map.131 = f32[8,128]{1,0:T(8,128)} custom-call(bf16[2,1024]{1,0:T(2,128)(2,1)} %q_hbm.1, bf16[1024,128]{1,0:T(8,128)(2,1)} %k_hbm.1, bf16[1024,128]{1,0:T(8,128)(2,1)} %v_hbm.1, bf16[2,128]{1,0:T(2,128)(2,1)} %rk_hbm.1, bf16[2,128]{1,0:T(2,128)(2,1)} %rv_hbm.1, s32[1]{0:T(128)S(6)} %copy.14.bp_hbm, s32[4]{0:T(128)} %len_hbm.1, ...), custom_call_target="tpu_custom_call" | custom-call | tf_op jit(solution)/shard_map/pallas_call | solution.py:451
  60.1 1.5 %slice_reduce_fusion = (f32[2]{0:T(128)}, f32[2]{0:T(128)}) fusion(f32[8,128]{1,0:T(8,128)} %shard_map.131), kind=kLoop, calls=%fused_computation | loop fusion | bytes 32 | tf_op jit(solution)/shard_map/slice | solution.py:507

commit v4 on v3

--- a/solution.py
+++ b/solution.py
@@ -216,20 +216,19 @@
         row = 4 * (n // 16) + 2 * core + n % 2
         row_segment = segment(row)
         row_prompt = (row_segment // 2).astype(F32)
-        parts = []
+        allowed = (lane < 4) & (key_segment == row_segment) & (key_row <= row)
+        reply = jnp.where(allowed, dot_t(q, rk), NEG)
+        scores = [dot_t(q, kbuf[block]) for block in range(2)]
+        reply_top = jnp.max(reply, axis=1, keepdims=True)
+        tops = [jnp.max(s, axis=1, keepdims=True) for s in scores]
+        p = jnp.where(allowed, jnp.exp2((reply - reply_top) * c1), 0.0)
+        parts = [(reply_top, jnp.sum(p, axis=1, keepdims=True), dot(p.astype(BF16), rv))]
         for block in range(2):
-            s = dot_t(q, kbuf[block])
-            m = jnp.max(s, axis=1, keepdims=True)
-            p = jnp.exp2((s - m) * c1)
+            p = jnp.exp2((scores[block] - tops[block]) * c1)
             total = jnp.sum(p, axis=1, keepdims=True)
             acc = dot(p.astype(BF16), vbuf[block])
-            m = jnp.where(row_prompt == prompts[block], m, NEG)
+            m = jnp.where(row_prompt == prompts[block], tops[block], NEG)
             parts.append((m, total, acc))
-        allowed = (lane < 4) & (key_segment == row_segment) & (key_row <= row)
-        s = jnp.where(allowed, dot_t(q, rk), NEG)
-        m = jnp.max(s, axis=1, keepdims=True)
-        p = jnp.where(allowed, jnp.exp2((s - m) * c1), 0.0)
-        parts.append((m, jnp.sum(p, axis=1, keepdims=True), dot(p.astype(BF16), rv)))
         top = jnp.maximum(jnp.maximum(parts[0][0], parts[1][0]), parts[2][0])
         total = jnp.zeros((CHUNK, LANES), F32)
         acc = jnp.zeros((CHUNK, HD), F32)

time: 61.8 us -> 60.2 us (0.974)
  Pallas kernels: 58.8 us -> 57.3 us
    pallas_call x1, Pallas kernels: 58.8 us -> 57.3 us  [body(): pl.pallas_call(functools.partial(kernel, plane, ny, width), out_shape=jax...]
where the time goes in v4:
time: 60.2 us; the launch traced here: 60.1 us
  Pallas kernels  57.3 us (95%)
  local copies, waits for them, and re-layouts  1.49 us (2%)
  between operations  1.29 us (2%)
    pallas_call x1, Pallas kernels, body(): pl.pallas_call(functools.partial(kernel, plane, ny, width), out_shape=jax...  57.3 us
    slice x1, local copies, waits for them, and re-layouts, body(): return (out[0:2, 0], out[0:2, 64])  1.49 us

profile of v4, /device:TPU:8, one launch (start us, length us, event | category | flops | bytes accessed | tf_op | source)
XLA Modules:
  0.0 60.1 jit_solution(13538468075814526755)
XLA Ops:
  1.3 57.3 %shard_map.131 = f32[8,128]{1,0:T(8,128)} custom-call(bf16[2,1024]{1,0:T(2,128)(2,1)} %q_hbm.1, bf16[1024,128]{1,0:T(8,128)(2,1)} %k_hbm.1, bf16[1024,128]{1,0:T(8,128)(2,1)} %v_hbm.1, bf16[2,128]{1,0:T(2,128)(2,1)} %rk_hbm.1, bf16[2,128]{1,0:T(2,128)(2,1)} %rv_hbm.1, s32[1]{0:T(128)S(6)} %copy.14.bp_hbm, s32[4]{0:T(128)} %len_hbm.1, ...), custom_call_target="tpu_custom_call" | custom-call | tf_op jit(solution)/shard_map/pallas_call | solution.py:450
  58.6 1.5 %slice_reduce_fusion = (f32[2]{0:T(128)}, f32[2]{0:T(128)}) fusion(f32[8,128]{1,0:T(8,128)} %shard_map.131), kind=kLoop, calls=%fused_computation | loop fusion | bytes 32 | tf_op jit(solution)/shard_map/slice | solution.py:506
